TPU v7x, 32 devices: a whole 2x2x4 slice. The times are simulated.
32 devices in a mesh: groups: 2 (over y), bank: 8 (over z, x), clus: 2 (over core).
Axes of the slice: x: 2, y: 2, z: 4, core: 2. Of those that a mesh axis runs over, the one named last changes fastest.
Arguments:
- features: bfloat16 [6144, 768], P(('groups', 'bank'), 'clus'), parts along dimension 0, may hold values from -6 to 6
- cluster_ids: int32 [6144], P(('groups', 'bank')), parts along dimension 0, may hold values from 0 to 4095, as said below
- w_in: bfloat16 [768, 1536], P(None, 'clus'), may hold values from -0.21875 to 0.21875
- w_out: bfloat16 [1536, 768], P('clus'), may hold values from -0.15625 to 0.15625
- old_centroids: bfloat16 [8192, 768], P(('groups', 'bank'), 'clus'), parts along dimension 0, may hold values from -6 to 6
Outputs:
- centroids: bfloat16 [8192, 768], P(('groups', 'bank')), parts along dimension 0
There are 2 independent parts, one for each index of `groups`. A program takes and returns all parts, laid end to end along the dimension named above; an argument that names none is the same for every part. Nothing has to cross between parts.
Inputs may be any that keep to these rules, and one draw needn't show every extreme that they name: `cluster_ids`: cluster k is owned by bank index k // 512. The rows of one bank index name clusters of one owner at most 144 times, and one owner, drawn from the seed, receives exactly 144 rows from every bank index.
All inputs are finite; a program needn't handle non-finite values.
Results may differ from a plain program's by a relative error of at most 0.0035.
Values may be sent and summed in bfloat16 or wider, within the bound.
A program may use at most 64 MiB of HBM per device.

v0:
```python
import jax
import jax.numpy as jnp
from jax import lax
from jax.sharding import PartitionSpec as P

D = 768
CL_DEV = 512


epsilon = 1e-06


def route_and_sum(row_keys, row_ids, capacity):
    n_bank = lax.axis_size("bank")
    count_rows = row_keys.shape[0]
    width = row_keys.shape[1]
    owners = row_ids // CL_DEV
    dest_table = (owners[:, None] == jnp.arange(n_bank, dtype=jnp.int32)[None, :]).astype(
        jnp.bfloat16
    )
    positions = jnp.arange(count_rows, dtype=jnp.int32)
    earlier = (positions[:, None] > positions[None, :]).astype(jnp.bfloat16)
    before = jnp.dot(earlier, dest_table, preferred_element_type=jnp.float32)
    rank_in = jnp.sum(before * dest_table.astype(jnp.float32), axis=1).astype(jnp.int32)
    slot_index = owners * capacity + rank_in
    send_rows = jnp.zeros((n_bank * capacity, width), jnp.bfloat16).at[slot_index].set(row_keys)
    send_ids = jnp.full((n_bank * capacity,), -1, jnp.int32).at[slot_index].set(row_ids)
    send_rows = send_rows.reshape(n_bank, capacity, width)
    send_ids = send_ids.reshape(n_bank, capacity)
    recv_rows, recv_ids = (
        lax.all_to_all(send_rows, "bank", split_axis=0, concat_axis=0, tiled=True),
        lax.all_to_all(send_ids, "bank", split_axis=0, concat_axis=0, tiled=True),
    )
    local_ids = recv_ids.reshape(-1) - lax.axis_index("bank") * CL_DEV
    member = (jnp.arange(CL_DEV, dtype=jnp.int32)[:, None] == local_ids[None, :]).astype(
        jnp.bfloat16
    )
    cluster_sums = jnp.dot(member, recv_rows.reshape(-1, width), preferred_element_type=jnp.float32)
    counts = jnp.sum(member, axis=1, dtype=jnp.float32)
    return (cluster_sums, counts)


def shards(features, cluster_ids, w_in, w_out, old_centroids):
    n_bank = lax.axis_size("bank")
    count_rows = features.shape[0]
    capacity = 3 * count_rows // n_bank
    whole_rows = lax.all_gather(features, "clus", axis=1, tiled=True)
    hidden = jax.nn.gelu(jnp.dot(whole_rows, w_in, preferred_element_type=jnp.float32)).astype(
        jnp.bfloat16
    )
    partial_value = jnp.dot(hidden, w_out, preferred_element_type=jnp.float32)
    branch = lax.psum_scatter(partial_value, "clus", scatter_dimension=1, tiled=True)
    residual = features.astype(jnp.float32) + branch
    squares = lax.psum(jnp.sum(residual * residual, axis=1, keepdims=True), "clus")
    row_keys = (residual * lax.rsqrt(squares / D + epsilon)).astype(jnp.bfloat16)
    cluster_sums, counts = route_and_sum(row_keys, cluster_ids, capacity)
    pooled = (cluster_sums + old_centroids.astype(jnp.float32)) / (counts[:, None] + 1.0)
    squares = lax.psum(jnp.sum(pooled * pooled, axis=1, keepdims=True), "clus")
    scaled = (pooled * lax.rsqrt(squares / D + epsilon)).astype(jnp.bfloat16)
    return lax.all_gather(scaled, "clus", axis=1, tiled=True)


def solution(mesh):
    placed = (
        P(("groups", "bank"), "clus"),
        P(("groups", "bank")),
        P(None, "clus"),
        P("clus", None),
        P(("groups", "bank"), "clus"),
    )
    return jax.shard_map(
        shards, mesh=mesh, in_specs=placed, out_specs=P(("groups", "bank"), None), check_vma=False
    )
```

profile of v0, /device:TPU:0, one launch (start us, length us, event | category | flops | bytes accessed | tf_op | source)
XLA Modules:
  0.0 73.8 jit_solution(14190300939445475012)
XLA Ops:
  6.5 0.0 copy-start
  6.5 0.0 reduce-scatter.2.cloned.1.call-start
  6.5 2.6 %all_gather.6 = bf16[384,768]{1,0:T(8,128)(2,1)S(1)} all-gather(bf16[384,384]{1,0:T(8,128)(2,1)} %param.5), channel_id=1, replica_groups=mesh['groups'=2,'bank'=8,'clus'=2] {'clus'}, dimensions={1}, use_global_device_ids=true | all-gather | bytes 884736 | tf_op jit(solution)/shard_map/all_gather | solution.py:47
  9.2 0.0 copy-done
  9.2 3.5 %fusion.14 = f32[384,768]{1,0:T(8,128)} fusion(bf16[768,768]{1,0:T(8,128)(2,1)S(1)} %copy-done, bf16[384,768]{1,0:T(8,128)(2,1)S(1)} %all_gather.6, bf16[768,768]{1,0:T(8,128)(2,1)} %param.7), kind=kOutput, calls=%fused_computation.22 | convolution fusion | flops 908623872 | bytes 4128768 | tf_op jit(solution)/shard_map/dot_general | solution.py:51
  12.7 0.0 copy-start.4
  12.7 0.0 copy-start.1
  12.7 0.0 reduce-scatter.2.cloned.1.call-update
  12.8 0.7 copy-done.4
  13.4 0.2 fusion.13
  13.6 2.9 %scatter_custom_fusion = s32[1152]{0:T(1024)S(1)} fusion(s32[384]{0:T(512)S(1)} %compare_select_fusion, s32[384]{0:T(512)S(1)} %copy-done.4, s32[]{:T(128)} %constant.18.clone.1), kind=kCustom, calls=%fused_computation.39 | custom fusion | bytes 4612 | tf_op jit(solution)/shard_map/scatter | solution.py:27
  16.6 0.7 all_to_all.9
  17.3 7.2 %all-to-all-start = ((s32[8,1,144]{2,1,0:T(1,128)}), s32[8,1,144]{2,1,0:T(1,128)S(1)}, u32[]{:S(2)}, u32[]{:S(2)}) async-start(s32[8,1,144]{2,1,0:T(1,128)} %all_to_all.9), calls=%async_computation | async-start | bytes 16384 | tf_op jit(solution)/shard_map/all_to_all | solution.py:32
  24.4 0.0 reduce-scatter.2.cloned.1.call-done
  24.5 0.0 copy-done.1
  24.5 0.0 copy-start.2
  24.5 1.3 %multiply_reduce_fusion.1 = f32[384]{0:T(512)S(1)} fusion(f32[384,384]{1,0:T(8,128)} %reduce-scatter.2.cloned.1.call-done, bf16[384,384]{1,0:T(8,128)(2,1)S(1)} %copy-done.1), kind=kLoop, calls=%fused_computation.24 | loop fusion | flops 589440 | bytes 886272 | tf_op jit(solution)/shard_map/reduce_sum | solution.py:54
  25.8 2.5 %psum.14 = f32[384,1]{0,1:T(1,128)S(1)} all-reduce(f32[384,1]{0,1:T(1,128)S(1)} %broadcast_in_dim.26), channel_id=1, replica_groups=mesh['groups'=2,'bank'=8,'clus'=2] {'clus'}, use_global_device_ids=true, to_apply=%region_4.5 | all-reduce | flops 384 | bytes 3072 | tf_op jit(solution)/shard_map/psum | solution.py:54
  28.3 0.0 copy-done.2
  28.3 3.0 %scatter_custom_fusion.1 = bf16[1152,384]{1,0:T(8,128)(2,1)} fusion(s32[384]{0:T(512)S(1)} %compare_select_fusion, bf16[]{:T(256)} %constant.43.clone.1, f32[384,384]{1,0:T(8,128)S(1)} %copy-done.2, bf16[384,384]{1,0:T(8,128)(2,1)S(1)} %copy-done.1, f32[384]{0:T(512)S(1)} %rsqrt_reduce_fusion), kind=kCustom, calls=%fused_computation.31 | custom fusion | flops 589824 | bytes 1771522 | tf_op jit(solution)/shard_map/scatter | solution.py:26
  31.3 0.0 all-to-all-done
  31.3 6.1 %all-to-all-start.1 = ((bf16[8,144,384]{2,1,0:T(8,128)(2,1)}), bf16[8,144,384]{2,1,0:T(8,128)(2,1)S(1)}, u32[]{:S(2)}, u32[]{:S(2)}) async-start(bf16[8,144,384]{2,1,0:T(8,128)(2,1)} %bitcast), calls=%async_computation.2 | async-start | bytes 1769472 | tf_op jit(solution)/shard_map/all_to_all | solution.py:31
  37.4 0.0 copy-done.3
  37.4 0.2 copy.10
  37.7 0.1 sub.22
  37.7 0.3 convert_reduce_fusion
  38.1 21.9 %all-to-all-done.1 = bf16[8,144,384]{2,1,0:T(8,128)(2,1)S(1)} async-done(((bf16[8,144,384]{2,1,0:T(8,128)(2,1)}), bf16[8,144,384]{2,1,0:T(8,128)(2,1)S(1)}, u32[]{:S(2)}, u32[]{:S(2)}) %all-to-all-start.1) | async-done | bytes 884768 | tf_op jit(solution)/shard_map/all_to_all | solution.py:31
  60.0 0.8 %multiply_reduce_fusion = (f32[512]{0:T(512)S(1)}, f32[512,384]{0,1:T(8,128)S(1)}) fusion(f32[512]{0:T(512)S(1)} %broadcast_add_fusion, bf16[512,384]{0,1:T(8,128)(2,1)S(1)} %copy.10, bf16[1152,384]{1,0:T(8,128)(2,1)S(1)} %bitcast.8, s32[1152]{0:T(1024)S(1)} %sub.22), kind=kOutput, calls=%fused_computation.21 | convolution fusion | flops 454557184 | bytes 2073088 | tf_op jit(solution)/shard_map/dot_general | solution.py:38
  60.8 2.5 %psum.15 = f32[512,1]{0,1:T(1,128)S(1)} all-reduce(f32[512,1]{0,1:T(1,128)S(1)} %bitcast.10), channel_id=1, replica_groups=mesh['groups'=2,'bank'=8,'clus'=2] {'clus'}, use_global_device_ids=true, to_apply=%region_8.9 | all-reduce | flops 512 | bytes 4096 | tf_op jit(solution)/shard_map/psum | solution.py:58
  63.3 0.1 multiply_convert_fusion
  63.4 2.4 %all_gather.7 = bf16[512,768]{0,1:T(8,128)(2,1)S(1)} all-gather(bf16[512,384]{0,1:T(8,128)(2,1)S(1)} %multiply_convert_fusion), channel_id=1, replica_groups=mesh['groups'=2,'bank'=8,'clus'=2] {'clus'}, dimensions={1}, use_global_device_ids=true | all-gather | bytes 1179648 | tf_op jit(solution)/shard_map/all_gather | solution.py:60
  65.8 1.2 %copy.11 = bf16[512,768]{1,0:T(8,128)(2,1)} copy(bf16[512,768]{0,1:T(8,128)(2,1)S(1)} %all_gather.7) | data formatting | bytes 1572864 | tf_op jit(solution)/shard_map/all_gather | solution.py:60
  (8 shorter events, 0.1 us)
Async XLA Ops:
  6.5 2.6 %copy-start = (bf16[768,768]{1,0:T(8,128)(2,1)S(1)}, bf16[768,768]{1,0:T(8,128)(2,1)}, u32[]{:S(2)}) copy-start(bf16[768,768]{1,0:T(8,128)(2,1)} %param.8) | copy-start | bytes 3538948
  6.5 17.9 %reduce-scatter.2.cloned.1.call-start = ((), (), s32[]{:S(2)}) async-start(), calls=%async_computation.3 | async-start | bytes 1769472 | tf_op jit(solution)/shard_map/reduce_scatter | solution.py:52
  12.7 0.7 copy-start.4
  12.7 11.7 %copy-start.1 = (bf16[384,384]{1,0:T(8,128)(2,1)S(1)}, bf16[384,384]{1,0:T(8,128)(2,1)}, u32[]{:S(2)}) copy-start(bf16[384,384]{1,0:T(8,128)(2,1)} %param.5) | copy-start | bytes 884740
  17.3 14.0 %all-to-all-start = ((s32[8,1,144]{2,1,0:T(1,128)}), s32[8,1,144]{2,1,0:T(1,128)S(1)}, u32[]{:S(2)}, u32[]{:S(2)}) async-start(s32[8,1,144]{2,1,0:T(1,128)} %all_to_all.9), calls=%async_computation | async-start | bytes 16384 | tf_op jit(solution)/shard_map/all_to_all | solution.py:32
  24.5 3.8 %copy-start.2 = (f32[384,384]{1,0:T(8,128)S(1)}, f32[384,384]{1,0:T(8,128)}, u32[]{:S(2)}) copy-start(f32[384,384]{1,0:T(8,128)} %reduce-scatter.2.cloned.1.call-done) | copy-start | bytes 1769476
  31.3 6.1 %copy-start.3 = (bf16[512,384]{1,0:T(8,128)(2,1)S(1)}, bf16[512,384]{1,0:T(8,128)(2,1)}, u32[]{:S(2)}) copy-start(bf16[512,384]{1,0:T(8,128)(2,1)} %param.9) | copy-start | bytes 1179652
  31.3 28.7 %all-to-all-start.1 = ((bf16[8,144,384]{2,1,0:T(8,128)(2,1)}), bf16[8,144,384]{2,1,0:T(8,128)(2,1)S(1)}, u32[]{:S(2)}, u32[]{:S(2)}) async-start(bf16[8,144,384]{2,1,0:T(8,128)(2,1)} %bitcast), calls=%async_computation.2 | async-start | bytes 1769472 | tf_op jit(solution)/shard_map/all_to_all | solution.py:31
Sparse Core Ops, SparseCore 0:
  12.9 11.2 reduce-scatter.1
where the time goes:
time: 74.1 us; the launch traced here: 73.8 us
  waiting for transfers between devices  22 us (30%)
  between operations  13.5 us (18%)
  starting transfers between devices  13.3 us (18%)
  blocking collectives  9.95 us (13%)
  local copies, waits for them, and re-layouts  5.72 us (8%)
  other arithmetic  4.8 us (6%)
  matrix products  4.58 us (6%)
    all_to_all x1, waiting for transfers between devices, route_and_sum(): lax.all_to_all(send_rows, 'bank', split_axis=0, concat_axis=0, tiled=True)  21.9 us
    all_to_all x1, starting transfers between devices, route_and_sum(): lax.all_to_all(send_ids, 'bank', split_axis=0, concat_axis=0, tiled=True)  7.17 us
    all_to_all x1, starting transfers between devices, route_and_sum(): lax.all_to_all(send_rows, 'bank', split_axis=0, concat_axis=0, tiled=True)  6.1 us
    dot_general x1, matrix products, shards(): partial_value = jnp.dot(hidden, w_out, preferred_element_type=jnp.float32)  3.55 us
    scatter x1, other arithmetic, route_and_sum(): jnp.zeros((n_bank * capacity, width), jnp.bfloat16).at[slot_index]  3.02 us
    scatter x1, local copies, waits for them, and re-layouts, route_and_sum(): jnp.full((n_bank * capacity,), -1, jnp.int32).at[slot_index].set(row_ids)  2.93 us
    all_gather x1, blocking collectives, shards(): whole_rows = lax.all_gather(features, 'clus', axis=1, tiled=True)  2.64 us
    psum x1, blocking collectives, shards(): squares = lax.psum(jnp.sum(pooled * pooled, axis=1, keepdims=True), 'clus')  2.47 us
  transfers between devices with their start and end apart: 3, of which 1 were waited for; matrix products, arithmetic and copies ran while one was open for 11% of the time, Pallas kernels for 0%

commit v1 on v0

v1 whole, which is shorter than its diff:
```python
import functools

import jax
import jax.numpy as jnp
from jax import lax
from jax.experimental import pallas as pl
from jax.experimental.pallas import tpu as pltpu
from jax.sharding import PartitionSpec as P

D = 768
epsilon = 1e-06
BF16 = jnp.bfloat16
F32 = jnp.float32
MESH = pl.DeviceIdType.MESH


def dot(a, b):
    return jnp.dot(a, b, preferred_element_type=F32)


def each(low, high, body):
    if high - low <= 8:
        for d in range(low, high):
            body(d)
    else:

        def step(d, carry):
            body(d)
            return carry

        lax.fori_loop(low, high, step, 0)


def kernel(
    n, n_rows, n_out, features_in, ids_ref, w_in_in, w_out_in, old_in, out_ref,
    features, peer, w_in, w_out, old, hidden_sum, part, part_send, part_recv,
    sq_send, sq_recv, keys, pick, stage, recv, ids_send, ids_recv, member, counts, sums,
    fin_send, fin_recv, fin_half, load_sems, pair_send, pair_recv, part_s, part_r,
    sq_s, sq_r, ids_s, ids_r, row_s, row_r, fin_s, fin_r, half_s, half_r, own_s,
):
    group = lax.axis_index("groups")
    me = lax.axis_index("bank")
    core = lax.axis_index("clus")
    rows, half = features.shape
    owned = sums.shape[0]
    slots = recv.shape[1]
    row_block = rows // n_rows
    out_block = owned // n_out
    other = (group, me, 1 - core)

    def bank(d):
        return (group, lax.rem(me + d, n), core)

    def remote(src, dst, send, arrive, to):
        return pltpu.make_async_remote_copy(
            src_ref=src, dst_ref=dst, send_sem=send, recv_sem=arrive,
            device_id=to, device_id_type=MESH,
        )

    barrier = pltpu.get_barrier_semaphore()
    pl.semaphore_signal(barrier, inc=1, device_id=other, device_id_type=MESH)
    each(
        1, n,
        lambda d: pl.semaphore_signal(barrier, inc=1, device_id=bank(d), device_id_type=MESH),
    )
    loads = [
        pltpu.make_async_copy(src, dst, load_sems.at[i])
        for i, (src, dst) in enumerate(
            ((features_in, features), (w_in_in, w_in), (w_out_in, w_out), (old_in, old))
        )
    ]
    for load in loads:
        load.start()

    ids = ids_ref[...]
    owner = lax.div(ids, jnp.int32(owned))
    local = ids - owner * owned + 1
    owner_rows = max(16, n)
    table = jnp.where(
        lax.broadcasted_iota(jnp.int32, (owner_rows, rows), 0) == owner, 1.0, 0.0
    )
    earlier = jnp.where(
        lax.broadcasted_iota(jnp.int32, (rows, rows), 0)
        < lax.broadcasted_iota(jnp.int32, (rows, rows), 1),
        1.0, 0.0,
    ).astype(BF16)
    before = dot(table.astype(BF16), earlier)
    rank = jnp.sum(before * table, axis=0, keepdims=True).astype(jnp.int32)
    high = lax.div(local, jnp.int32(32))
    low = local - 32 * high
    digits = jnp.where(
        lax.broadcasted_iota(jnp.int32, (16, rows), 0) < 8, high, low
    ).astype(F32).astype(BF16)

    def place(d):
        to = lax.rem(me + d, n)
        slot = jnp.where(owner == to, rank, -1)
        chosen = jnp.where(
            lax.broadcasted_iota(jnp.int32, (slots, rows), 0) == slot, 1.0, 0.0
        ).astype(BF16)
        pick[d] = chosen
        found = lax.dot_general(
            digits, chosen, (((1,), (1,)), ((), ())), preferred_element_type=F32
        )
        ids_send[d, :, :slots] = (32.0 * found[:8] + found[8:] - 1.0).astype(jnp.int32)

    each(0, n, place)

    pl.semaphore_wait(barrier, n)
    loads[0].wait()
    to_peer = remote(features, peer, pair_send, pair_recv, other)
    to_peer.start()

    def id_copy(d):
        return remote(ids_send.at[d], ids_recv.at[d], ids_s.at[d], ids_r.at[d], bank(d))

    each(1, n, lambda d: id_copy(d).start())

    mine = pl.ds(pl.multiple_of(core * half, 128), half)
    theirs = pl.ds(pl.multiple_of((1 - core) * half, 128), half)
    loads[1].wait()
    hidden_sum[...] = dot(features[...], w_in[mine, :])
    loads[2].wait()
    to_peer.wait()
    part_copies = []
    for b in range(n_rows):
        block = slice(b * row_block, (b + 1) * row_block)
        hidden = jax.nn.gelu(
            hidden_sum[block, :] + dot(peer[block, :], w_in[theirs, :])
        ).astype(BF16)
        part_send[block, :] = dot(hidden, w_out[:, theirs])
        copy = remote(part_send.at[block], part_recv.at[block], part_s.at[b], part_r.at[b], other)
        copy.start()
        part_copies.append(copy)
        part[block, :] = features[block, :].astype(F32) + dot(hidden, w_out[:, mine])

    sq_copies = []
    for b in range(n_rows):
        block = slice(b * row_block, (b + 1) * row_block)
        part_copies[b].wait()
        residual = part[block, :] + part_recv[block, :]
        part[block, :] = residual
        sq_send[block, :] = jnp.broadcast_to(
            jnp.sum(residual * residual, axis=1, keepdims=True), (row_block, 128)
        )
        copy = remote(sq_send.at[block], sq_recv.at[block], sq_s.at[b], sq_r.at[b], other)
        copy.start()
        sq_copies.append(copy)
    for b in range(n_rows):
        block = slice(b * row_block, (b + 1) * row_block)
        sq_copies[b].wait()
        total = sq_send[block, :1] + sq_recv[block, :1]
        keys[block, :] = (part[block, :] * lax.rsqrt(total / D + epsilon)).astype(BF16)

    def row_copy(d):
        return remote(stage.at[d], recv.at[d], row_s.at[d], row_r.at[d], bank(d))

    def dispatch(d):
        stage[d] = dot(pick[d], keys[...]).astype(BF16)
        row_copy(d).start()

    each(1, n, dispatch)
    stage[0] = dot(pick[0], keys[...]).astype(BF16)

    def members(cluster_ids):
        found = jnp.where(
            lax.broadcasted_iota(jnp.int32, (owned, slots), 0) == cluster_ids, 1.0, 0.0
        )
        return found.astype(BF16), jnp.sum(found, axis=1, keepdims=True)

    own_member, own_count = members(ids_send[0, :1, :slots])
    counts[...] = jnp.broadcast_to(own_count, counts.shape)
    sums[...] = dot(own_member, stage[0])

    def match(d):
        id_copy(d).wait()
        chosen, count = members(ids_recv[d, :1, :slots])
        member[d] = chosen
        counts[...] += count

    each(1, n, match)
    loads[3].wait()

    def collect(d):
        row_copy(d).wait()
        sums[...] += dot(member[d], recv[d])

    each(1, n, collect)

    fin_copies = []
    for b in range(n_out):
        block = slice(b * out_block, (b + 1) * out_block)
        pooled = (sums[block, :] + old[block, :].astype(F32)) / (counts[block, :1] + 1.0)
        sums[block, :] = pooled
        fin_send[block, :] = jnp.broadcast_to(
            jnp.sum(pooled * pooled, axis=1, keepdims=True), (out_block, 128)
        )
        copy = remote(fin_send.at[block], fin_recv.at[block], fin_s.at[b], fin_r.at[b], other)
        copy.start()
        fin_copies.append(copy)
    half_copies = []
    for b in range(n_out):
        block = slice(b * out_block, (b + 1) * out_block)
        fin_copies[b].wait()
        total = fin_send[block, :1] + fin_recv[block, :1]
        fin_half[block, :] = (sums[block, :] * lax.rsqrt(total / D + epsilon)).astype(BF16)
        place_at = out_ref.at[block, mine]
        copy = remote(fin_half.at[block], place_at, half_s.at[b], half_r.at[b], other)
        copy.start()
        here = pltpu.make_async_copy(fin_half.at[block], place_at, own_s.at[b])
        here.start()
        half_copies += [copy, here]
    for copy in half_copies:
        copy.wait()


def shards(features, cluster_ids, w_in, w_out, old_centroids):
    n = lax.axis_size("bank")
    rows, half = features.shape
    hidden = w_in.shape[1]
    owned = old_centroids.shape[0]
    capacity = 3 * rows // n
    slots = -(-capacity // 16) * 16
    width = -(-slots // 128) * 128
    n_rows, n_out = 3, 4
    vmem, dma = pltpu.VMEM, pltpu.SemaphoreType.DMA
    anywhere = pl.BlockSpec(memory_space=pl.ANY)
    return pl.pallas_call(
        functools.partial(kernel, n, n_rows, n_out),
        out_shape=jax.ShapeDtypeStruct((owned, 2 * half), BF16),
        in_specs=[
            anywhere, pl.BlockSpec(memory_space=pltpu.VMEM), anywhere, anywhere, anywhere,
        ],
        out_specs=anywhere,
        scratch_shapes=[
            vmem((rows, half), BF16),
            vmem((rows, half), BF16),
            vmem(w_in.shape, BF16),
            vmem(w_out.shape, BF16),
            vmem((owned, half), BF16),
            vmem((rows, hidden), F32),
            vmem((rows, half), F32),
            vmem((rows, half), F32),
            vmem((rows, half), F32),
            vmem((rows, 128), F32),
            vmem((rows, 128), F32),
            vmem((rows, half), BF16),
            vmem((n, slots, rows), BF16),
            vmem((n, slots, half), BF16),
            vmem((n, slots, half), BF16),
            vmem((n, 8, width), jnp.int32),
            vmem((n, 8, width), jnp.int32),
            vmem((n, owned, slots), BF16),
            vmem((owned, 128), F32),
            vmem((owned, half), F32),
            vmem((owned, 128), F32),
            vmem((owned, 128), F32),
            vmem((owned, half), BF16),
            dma((4,)), dma, dma, dma((n_rows,)), dma((n_rows,)),
            dma((n_rows,)), dma((n_rows,)), dma((n,)), dma((n,)), dma((n,)), dma((n,)),
            dma((n_out,)), dma((n_out,)), dma((n_out,)), dma((n_out,)), dma((n_out,)),
        ],
        compiler_params=pltpu.CompilerParams(
            collective_id=0, has_side_effects=True, vmem_limit_bytes=50 * 1024 * 1024
        ),
    )(features, cluster_ids.reshape(1, rows), w_in, w_out, old_centroids)


def solution(mesh):
    placed = (
        P(("groups", "bank"), "clus"),
        P(("groups", "bank")),
        P(None, "clus"),
        P("clus", None),
        P(("groups", "bank"), "clus"),
    )
    return jax.shard_map(
        shards, mesh=mesh, in_specs=placed, out_specs=P(("groups", "bank"), None), check_vma=False
    )
```

time: 74.1 us -> 40.5 us (0.55)
  the two profiles are of different devices: /device:TPU:0 before, /device:TPU:27 now
where the time goes in v1:
time: 40.5 us; the launch traced here: 40.2 us
  Pallas kernels  34.2 us (84%)
  local copies, waits for them, and re-layouts  6.06 us (15%)
    pallas_call x1, Pallas kernels, shards(): pl.pallas_call(functools.partial(kernel, n, n_rows, n_out), out_shape=jax...  34.2 us
    unnamed x9, local copies, waits for them, and re-layouts  5.38 us

profile of v1, /device:TPU:27, one launch (start us, length us, event | category | flops | bytes accessed | tf_op | source)
XLA Modules:
  0.0 40.2 jit_solution(9785780500651559773)
XLA Ops:
  0.0 0.7 %reshape.3.ids_ref = s32[1,384]{1,0:T(1,128)S(1)} reshape(s32[384]{0:T(512)} %param.6) | data formatting | bytes 3072 | tf_op jit(solution)/shard_map/reshape | solution.py:266
  0.7 0.0 copy-start
  0.7 1.3 %copy-done = bf16[768,768]{1,0:T(8,128)(2,1)S(1)} copy-done((bf16[768,768]{1,0:T(8,128)(2,1)S(1)}, bf16[768,768]{1,0:T(8,128)(2,1)}, u32[]{:S(2)}) %copy-start) | copy-done | bytes 1179672
  2.0 0.0 copy-start.1
  2.0 1.3 %copy-done.1 = bf16[768,768]{1,0:T(8,128)(2,1)S(1)} copy-done((bf16[768,768]{1,0:T(8,128)(2,1)S(1)}, bf16[768,768]{1,0:T(8,128)(2,1)}, u32[]{:S(2)}) %copy-start.1) | copy-done | bytes 1179672
  3.2 0.0 copy-start.2
  3.2 1.0 %copy-done.2 = bf16[512,384]{1,0:T(8,128)(2,1)S(1)} copy-done((bf16[512,384]{1,0:T(8,128)(2,1)S(1)}, bf16[512,384]{1,0:T(8,128)(2,1)}, u32[]{:S(2)}) %copy-start.2) | copy-done | bytes 393240
  4.2 0.0 copy-start.3
  4.2 1.0 %copy-done.3 = bf16[384,384]{1,0:T(8,128)(2,1)S(1)} copy-done((bf16[384,384]{1,0:T(8,128)(2,1)S(1)}, bf16[384,384]{1,0:T(8,128)(2,1)}, u32[]{:S(2)}) %copy-start.3) | copy-done | bytes 294936
  5.2 34.2 %shard_map.55 = bf16[512,768]{1,0:T(8,128)(2,1)S(1)} custom-call(bf16[384,384]{1,0:T(8,128)(2,1)S(1)} %copy-done.3, s32[1,384]{1,0:T(1,128)S(1)} %reshape.3.ids_ref, bf16[768,768]{1,0:T(8,128)(2,1)S(1)} %copy-done, bf16[768,768]{1,0:T(8,128)(2,1)S(1)} %copy-done.1, bf16[512,384]{1,0:T(8,128)(2,1)S(1)} %copy-done.2), custom_call_target="tpu_custom_call" | custom-call | tf_op jit(solution)/shard_map/pallas_call | solution.py:228
  39.3 0.9 %copy.7 = bf16[512,768]{1,0:T(8,128)(2,1)} copy(bf16[512,768]{1,0:T(8,128)(2,1)S(1)} %shard_map.55) | data formatting | bytes 1572864
Async XLA Ops:
  0.7 1.3 %copy-start = (bf16[768,768]{1,0:T(8,128)(2,1)S(1)}, bf16[768,768]{1,0:T(8,128)(2,1)}, u32[]{:S(2)}) copy-start(bf16[768,768]{1,0:T(8,128)(2,1)} %w_in_in.1) | copy-start | bytes 3538948
  2.0 1.3 %copy-start.1 = (bf16[768,768]{1,0:T(8,128)(2,1)S(1)}, bf16[768,768]{1,0:T(8,128)(2,1)}, u32[]{:S(2)}) copy-start(bf16[768,768]{1,0:T(8,128)(2,1)} %w_out_in.1) | copy-start | bytes 3538948
  3.2 1.0 %copy-start.2 = (bf16[512,384]{1,0:T(8,128)(2,1)S(1)}, bf16[512,384]{1,0:T(8,128)(2,1)}, u32[]{:S(2)}) copy-start(bf16[512,384]{1,0:T(8,128)(2,1)} %old_in.1) | copy-start | bytes 1179652
  4.2 1.0 %copy-start.3 = (bf16[384,384]{1,0:T(8,128)(2,1)S(1)}, bf16[384,384]{1,0:T(8,128)(2,1)}, u32[]{:S(2)}) copy-start(bf16[384,384]{1,0:T(8,128)(2,1)} %features_in.1) | copy-start | bytes 884740

commit v2 on v1

--- a/solution.py
+++ b/solution.py
@@ -72,7 +72,7 @@
     for load in loads:
         load.start()
 
-    ids = ids_ref[...]
+    ids = ids_ref[...].reshape(1, rows)
     owner = lax.div(ids, jnp.int32(owned))
     local = ids - owner * owned + 1
     owner_rows = max(16, n)
@@ -225,11 +225,12 @@
     n_rows, n_out = 3, 4
     vmem, dma = pltpu.VMEM, pltpu.SemaphoreType.DMA
     anywhere = pl.BlockSpec(memory_space=pl.ANY)
+    far = pl.BlockSpec(memory_space=pltpu.HBM)
     return pl.pallas_call(
         functools.partial(kernel, n, n_rows, n_out),
         out_shape=jax.ShapeDtypeStruct((owned, 2 * half), BF16),
         in_specs=[
-            anywhere, pl.BlockSpec(memory_space=pltpu.VMEM), anywhere, anywhere, anywhere,
+            far, pl.BlockSpec(memory_space=pltpu.VMEM), far, far, far,
         ],
         out_specs=anywhere,
         scratch_shapes=[
@@ -263,7 +264,13 @@
         compiler_params=pltpu.CompilerParams(
             collective_id=0, has_side_effects=True, vmem_limit_bytes=50 * 1024 * 1024
         ),
-    )(features, cluster_ids.reshape(1, rows), w_in, w_out, old_centroids)
+    )(
+        pltpu.with_memory_space_constraint(features, pltpu.HBM),
+        cluster_ids,
+        pltpu.with_memory_space_constraint(w_in, pltpu.HBM),
+        pltpu.with_memory_space_constraint(w_out, pltpu.HBM),
+        pltpu.with_memory_space_constraint(old_centroids, pltpu.HBM),
+    )
 
 
 def solution(mesh):

time: 40.5 us -> 35.9 us (0.89)
  local copies, waits for them, and re-layouts: 6.06 us -> 1.56 us
    unnamed x9 -> x3, local copies, waits for them, and re-layouts: 5.38 us -> 1.56 us
    reshape x1 -> x0, local copies, waits for them, and re-layouts: 0.68 us -> none  [shards(): cluster_ids.reshape(1, rows)]
where the time goes in v2:
time: 35.9 us; the launch traced here: 35.7 us
  Pallas kernels  34.2 us (95%)
  local copies, waits for them, and re-layouts  1.56 us (4%)
    pallas_call x1, Pallas kernels, shards(): pl.pallas_call(functools.partial(kernel, n, n_rows, n_out), out_shape=jax...  34.2 us
    unnamed x3, local copies, waits for them, and re-layouts  1.56 us

profile of v2, /device:TPU:27, one launch (start us, length us, event | category | flops | bytes accessed | tf_op | source)
XLA Modules:
  0.0 35.7 jit_solution(11391730803188555154)
XLA Ops:
  0.0 0.0 copy-start
  0.0 0.7 %copy-done = s32[384]{0:T(512)S(1)} copy-done((s32[384]{0:T(512)S(1)}, s32[384]{0:T(512)}, u32[]{:S(2)}) %copy-start) | copy-done | bytes 1560
  0.7 34.2 %shard_map.55 = bf16[512,768]{1,0:T(8,128)(2,1)S(1)} custom-call(bf16[384,384]{1,0:T(8,128)(2,1)} %features_in.1, s32[384]{0:T(512)S(1)} %copy-done, bf16[768,768]{1,0:T(8,128)(2,1)} %w_in_in.1, bf16[768,768]{1,0:T(8,128)(2,1)} %w_out_in.1, bf16[512,384]{1,0:T(8,128)(2,1)} %old_in.1), custom_call_target="tpu_custom_call" | custom-call | tf_op jit(solution)/shard_map/pallas_call | solution.py:229
  34.8 0.9 %copy.7 = bf16[512,768]{1,0:T(8,128)(2,1)} copy(bf16[512,768]{1,0:T(8,128)(2,1)S(1)} %shard_map.55) | data formatting | bytes 1572864
Async XLA Ops:
  0.0 0.7 %copy-start = (s32[384]{0:T(512)S(1)}, s32[384]{0:T(512)}, u32[]{:S(2)}) copy-start(s32[384]{0:T(512)} %ids_ref.1) | copy-start | bytes 4612

commit v3 on v2

--- a/solution.py
+++ b/solution.py
@@ -33,10 +33,10 @@
 
 def kernel(
     n, n_rows, n_out, features_in, ids_ref, w_in_in, w_out_in, old_in, out_ref,
-    features, peer, w_in, w_out, old, hidden_sum, part, part_send, part_recv,
-    sq_send, sq_recv, keys, pick, stage, recv, ids_send, ids_recv, member, counts, sums,
+    features, peer, w_in, w_out, old, hidden_sum, hidden, part, part_send, part_recv,
+    sq_send, sq_recv, keys, pick, stage_lead, recv_lead, stage, recv, ids_send, ids_recv, member, counts, sums, scale_send, scale_recv,
     fin_send, fin_recv, fin_half, load_sems, pair_send, pair_recv, part_s, part_r,
-    sq_s, sq_r, ids_s, ids_r, row_s, row_r, fin_s, fin_r, half_s, half_r, own_s,
+    sq_s, sq_r, ids_s, ids_r, lead_s, lead_r, scale_s, scale_r, row_s, row_r, fin_s, fin_r, half_s, half_r, own_s,
 ):
     group = lax.axis_index("groups")
     me = lax.axis_index("bank")
@@ -122,68 +122,135 @@
     hidden_sum[...] = dot(features[...], w_in[mine, :])
     loads[2].wait()
     to_peer.wait()
-    part_copies = []
+    lead = recv_lead.shape[2]
+    front, back = slice(0, lead), slice(lead, half)
+
+    def columns(first, width, own):
+        base = core if own else 1 - core
+        return pl.ds(pl.multiple_of(base * half + first, 128), width)
+
+    lead_copies = []
     for b in range(n_rows):
         block = slice(b * row_block, (b + 1) * row_block)
-        hidden = jax.nn.gelu(
+        hidden[block, :] = jax.nn.gelu(
             hidden_sum[block, :] + dot(peer[block, :], w_in[theirs, :])
         ).astype(BF16)
-        part_send[block, :] = dot(hidden, w_out[:, theirs])
-        copy = remote(part_send.at[block], part_recv.at[block], part_s.at[b], part_r.at[b], other)
+        part_send[block, front] = dot(hidden[block, :], w_out[:, columns(0, lead, False)])
+        copy = remote(
+            part_send.at[block, front], part_recv.at[block, front],
+            part_s.at[b], part_r.at[b], other,
+        )
         copy.start()
-        part_copies.append(copy)
-        part[block, :] = features[block, :].astype(F32) + dot(hidden, w_out[:, mine])
-
-    sq_copies = []
-    for b in range(n_rows):
-        block = slice(b * row_block, (b + 1) * row_block)
-        part_copies[b].wait()
-        residual = part[block, :] + part_recv[block, :]
-        part[block, :] = residual
-        sq_send[block, :] = jnp.broadcast_to(
-            jnp.sum(residual * residual, axis=1, keepdims=True), (row_block, 128)
-        )
-        copy = remote(sq_send.at[block], sq_recv.at[block], sq_s.at[b], sq_r.at[b], other)
-        copy.start()
-        sq_copies.append(copy)
-    for b in range(n_rows):
-        block = slice(b * row_block, (b + 1) * row_block)
-        sq_copies[b].wait()
-        total = sq_send[block, :1] + sq_recv[block, :1]
-        keys[block, :] = (part[block, :] * lax.rsqrt(total / D + epsilon)).astype(BF16)
+        lead_copies.append(copy)
+    part_send[:, back] = dot(hidden[...], w_out[:, columns(lead, half - lead, False)])
+    rest_copy = remote(
+        part_send.at[:, back], part_recv.at[:, back],
+        part_s.at[n_rows], part_r.at[n_rows], other,
+    )
+    rest_copy.start()
+    part[:, front] = features[:, front].astype(F32) + dot(
+        hidden[...], w_out[:, columns(0, lead, True)]
+    )
+    for copy in lead_copies:
+        copy.wait()
+    lead_residual = part[:, front] + part_recv[:, front]
+    keys[:, front] = lead_residual.astype(BF16)
+
+    def lead_rows(d):
+        return remote(
+            stage_lead.at[d], recv_lead.at[d], lead_s.at[d], lead_r.at[d], bank(d)
+        )
+
+    def dispatch_lead(d):
+        stage_lead[d] = dot(pick[d], keys[:, front]).astype(BF16)
+        lead_rows(d).start()
+
+    each(1, n, dispatch_lead)
+
+    part[:, back] = features[:, back].astype(F32) + dot(
+        hidden[...], w_out[:, columns(lead, half - lead, True)]
+    )
+    lead_squares = jnp.sum(lead_residual * lead_residual, axis=1, keepdims=True)
+    rest_copy.wait()
+    residual = part[:, back] + part_recv[:, back]
+    part[:, back] = residual
+    squares = lead_squares + jnp.sum(residual * residual, axis=1, keepdims=True)
+    sq_send[...] = jnp.transpose(jnp.broadcast_to(squares, (rows, 128)))[:8]
+    sq_copy = remote(sq_send, sq_recv, sq_s, sq_r, other)
+    sq_copy.start()
+    sq_copy.wait()
+    scale = lax.rsqrt((sq_send[...] + sq_recv[...]) / D + epsilon)
+    column = jnp.transpose(jnp.broadcast_to(scale[:1], (128, rows)))[:, :1]
+    keys[:, back] = (part[:, back] * column).astype(BF16)
+    coarse = scale.astype(BF16)
+    fine = (scale - coarse.astype(F32)).astype(BF16)
+    pieces = jnp.concatenate([coarse.astype(F32), fine.astype(F32)], axis=0).astype(BF16)
+
+    def scale_copy(d):
+        return remote(
+            scale_send.at[d], scale_recv.at[d], scale_s.at[d], scale_r.at[d], bank(d)
+        )
+
+    def slot_scales(d):
+        found = lax.dot_general(
+            pieces, pick[d], (((1,), (1,)), ((), ())), preferred_element_type=F32
+        )
+        scale_send[d, :1, :slots] = found[:1]
+        scale_send[d, 1:, :slots] = found[8:9]
 
     def row_copy(d):
-        return remote(stage.at[d], recv.at[d], row_s.at[d], row_r.at[d], bank(d))
+        return remote(
+            stage.at[d], recv.at[d], row_s.at[d], row_r.at[d], bank(d)
+        )
 
     def dispatch(d):
-        stage[d] = dot(pick[d], keys[...]).astype(BF16)
+        stage[d] = dot(pick[d], keys[:, back]).astype(BF16)
         row_copy(d).start()
 
+    def dispatch_scales(d):
+        slot_scales(d)
+        scale_copy(d).start()
+
+    each(1, n, dispatch_scales)
     each(1, n, dispatch)
-    stage[0] = dot(pick[0], keys[...]).astype(BF16)
-
-    def members(cluster_ids):
-        found = jnp.where(
-            lax.broadcasted_iota(jnp.int32, (owned, slots), 0) == cluster_ids, 1.0, 0.0
-        )
-        return found.astype(BF16), jnp.sum(found, axis=1, keepdims=True)
-
-    own_member, own_count = members(ids_send[0, :1, :slots])
-    counts[...] = jnp.broadcast_to(own_count, counts.shape)
-    sums[...] = dot(own_member, stage[0])
+    stage[0] = dot(pick[0], keys[:, back]).astype(BF16)
+    stage_lead[0] = dot(pick[0], keys[:, front]).astype(BF16)
+    slot_scales(0)
+
+    def matches(cluster_ids):
+        return lax.broadcasted_iota(jnp.int32, (owned, slots), 0) == cluster_ids
+
+    def lead_sum(found, scales, rows_in):
+        return dot(jnp.where(found, scales[:1, :slots], 0.0).astype(BF16), rows_in) + dot(
+            jnp.where(found, scales[1:, :slots], 0.0).astype(BF16), rows_in
+        )
+
+    found = matches(ids_send[0, :1, :slots])
+    ones = jnp.where(found, 1.0, 0.0)
+    counts[...] = jnp.broadcast_to(jnp.sum(ones, axis=1, keepdims=True), counts.shape)
+    sums[:, back] = dot(ones.astype(BF16), stage[0])
+    sums[:, front] = lead_sum(found, scale_send[0], stage_lead[0])
 
     def match(d):
         id_copy(d).wait()
-        chosen, count = members(ids_recv[d, :1, :slots])
-        member[d] = chosen
-        counts[...] += count
+        chosen = jnp.where(matches(ids_recv[d, :1, :slots]), 1.0, 0.0)
+        member[d] = chosen.astype(BF16)
+        counts[...] += jnp.sum(chosen, axis=1, keepdims=True)
 
     each(1, n, match)
+
+    def collect_lead(d):
+        lead_rows(d).wait()
+        scale_copy(d).wait()
+        found = matches(ids_recv[d, :1, :slots])
+        sums[:, front] += lead_sum(found, scale_recv[d], recv_lead[d])
+
+    each(1, n, collect_lead)
     loads[3].wait()
 
     def collect(d):
         row_copy(d).wait()
-        sums[...] += dot(member[d], recv[d])
+        sums[:, back] += dot(member[d], recv[d])
 
     each(1, n, collect)
 
@@ -223,6 +290,7 @@
     slots = -(-capacity // 16) * 16
     width = -(-slots // 128) * 128
     n_rows, n_out = 3, 4
+    lead = 128
     vmem, dma = pltpu.VMEM, pltpu.SemaphoreType.DMA
     anywhere = pl.BlockSpec(memory_space=pl.ANY)
     far = pl.BlockSpec(memory_space=pltpu.HBM)
@@ -240,25 +308,30 @@
             vmem(w_out.shape, BF16),
             vmem((owned, half), BF16),
             vmem((rows, hidden), F32),
+            vmem((rows, hidden), BF16),
             vmem((rows, half), F32),
             vmem((rows, half), F32),
             vmem((rows, half), F32),
-            vmem((rows, 128), F32),
-            vmem((rows, 128), F32),
+            vmem((8, rows), F32),
+            vmem((8, rows), F32),
             vmem((rows, half), BF16),
             vmem((n, slots, rows), BF16),
-            vmem((n, slots, half), BF16),
-            vmem((n, slots, half), BF16),
+            vmem((n, slots, lead), BF16),
+            vmem((n, slots, lead), BF16),
+            vmem((n, slots, half - lead), BF16),
+            vmem((n, slots, half - lead), BF16),
             vmem((n, 8, width), jnp.int32),
             vmem((n, 8, width), jnp.int32),
             vmem((n, owned, slots), BF16),
             vmem((owned, 128), F32),
             vmem((owned, half), F32),
+            vmem((n, 2, width), F32),
+            vmem((n, 2, width), F32),
             vmem((owned, 128), F32),
             vmem((owned, 128), F32),
             vmem((owned, half), BF16),
-            dma((4,)), dma, dma, dma((n_rows,)), dma((n_rows,)),
-            dma((n_rows,)), dma((n_rows,)), dma((n,)), dma((n,)), dma((n,)), dma((n,)),
+            dma((4,)), dma, dma, dma((n_rows + 1,)), dma((n_rows + 1,)), dma, dma,
+            dma((n,)), dma((n,)), dma((n,)), dma((n,)), dma((n,)), dma((n,)), dma((n,)), dma((n,)),
             dma((n_out,)), dma((n_out,)), dma((n_out,)), dma((n_out,)), dma((n_out,)),
         ],
         compiler_params=pltpu.CompilerParams(

time: 35.9 us -> 34.4 us (0.958)
  Pallas kernels: 34.2 us -> 32.7 us
    pallas_call x1, Pallas kernels: 34.2 us -> 32.7 us  [shards(): pl.pallas_call(functools.partial(kernel, n, n_rows, n_out), out_shape=jax...]
where the time goes in v3:
time: 34.4 us; the launch traced here: 34.2 us
  Pallas kernels  32.7 us (95%)
  local copies, waits for them, and re-layouts  1.56 us (5%)
    pallas_call x1, Pallas kernels, shards(): pl.pallas_call(functools.partial(kernel, n, n_rows, n_out), out_shape=jax...  32.7 us
    unnamed x3, local copies, waits for them, and re-layouts  1.56 us

profile of v3, /device:TPU:27, one launch (start us, length us, event | category | flops | bytes accessed | tf_op | source)
XLA Modules:
  0.0 34.2 jit_solution(15082783143465850270)
XLA Ops:
  0.0 0.0 copy-start
  0.0 0.7 %copy-done = s32[384]{0:T(512)S(1)} copy-done((s32[384]{0:T(512)S(1)}, s32[384]{0:T(512)}, u32[]{:S(2)}) %copy-start) | copy-done | bytes 1560
  0.7 32.7 %shard_map.55 = bf16[512,768]{1,0:T(8,128)(2,1)S(1)} custom-call(bf16[384,384]{1,0:T(8,128)(2,1)} %features_in.1, s32[384]{0:T(512)S(1)} %copy-done, bf16[768,768]{1,0:T(8,128)(2,1)} %w_in_in.1, bf16[768,768]{1,0:T(8,128)(2,1)} %w_out_in.1, bf16[512,384]{1,0:T(8,128)(2,1)} %old_in.1), custom_call_target="tpu_custom_call" | custom-call | tf_op jit(solution)/shard_map/pallas_call | solution.py:297
  33.4 0.9 %copy.7 = bf16[512,768]{1,0:T(8,128)(2,1)} copy(bf16[512,768]{1,0:T(8,128)(2,1)S(1)} %shard_map.55) | data formatting | bytes 1572864
Async XLA Ops:
  0.0 0.7 %copy-start = (s32[384]{0:T(512)S(1)}, s32[384]{0:T(512)}, u32[]{:S(2)}) copy-start(s32[384]{0:T(512)} %ids_ref.1) | copy-start | bytes 4612

commit v4 on v3

--- a/solution.py
+++ b/solution.py
@@ -108,8 +108,12 @@
 
     pl.semaphore_wait(barrier, n)
     loads[0].wait()
-    to_peer = remote(features, peer, pair_send, pair_recv, other)
-    to_peer.start()
+    to_peer = []
+    for b in range(n_rows):
+        block = slice(b * row_block, (b + 1) * row_block)
+        copy = remote(features.at[block], peer.at[block], pair_send.at[b], pair_recv.at[b], other)
+        copy.start()
+        to_peer.append(copy)
 
     def id_copy(d):
         return remote(ids_send.at[d], ids_recv.at[d], ids_s.at[d], ids_r.at[d], bank(d))
@@ -121,7 +125,6 @@
     loads[1].wait()
     hidden_sum[...] = dot(features[...], w_in[mine, :])
     loads[2].wait()
-    to_peer.wait()
     lead = recv_lead.shape[2]
     front, back = slice(0, lead), slice(lead, half)
 
@@ -132,6 +135,7 @@
     lead_copies = []
     for b in range(n_rows):
         block = slice(b * row_block, (b + 1) * row_block)
+        to_peer[b].wait()
         hidden[block, :] = jax.nn.gelu(
             hidden_sum[block, :] + dot(peer[block, :], w_in[theirs, :])
         ).astype(BF16)
@@ -330,7 +334,7 @@
             vmem((owned, 128), F32),
             vmem((owned, 128), F32),
             vmem((owned, half), BF16),
-            dma((4,)), dma, dma, dma((n_rows + 1,)), dma((n_rows + 1,)), dma, dma,
+            dma((4,)), dma((n_rows,)), dma((n_rows,)), dma((n_rows + 1,)), dma((n_rows + 1,)), dma, dma,
             dma((n,)), dma((n,)), dma((n,)), dma((n,)), dma((n,)), dma((n,)), dma((n,)), dma((n,)),
             dma((n_out,)), dma((n_out,)), dma((n_out,)), dma((n_out,)), dma((n_out,)),
         ],

time: 34.4 us -> 34.2 us (level)
  no operation moved by 1% of the time
where the time goes in v4:
time: 34.2 us; the launch traced here: 34 us
  Pallas kernels  32.5 us (95%)
  local copies, waits for them, and re-layouts  1.56 us (5%)
    pallas_call x1, Pallas kernels, shards(): pl.pallas_call(functools.partial(kernel, n, n_rows, n_out), out_shape=jax...  32.5 us
    unnamed x3, local copies, waits for them, and re-layouts  1.56 us

profile of v4, /device:TPU:27, one launch (start us, length us, event | category | flops | bytes accessed | tf_op | source)
XLA Modules:
  0.0 34.0 jit_solution(7095724376715148673)
XLA Ops:
  0.0 0.0 copy-start
  0.0 0.7 %copy-done = s32[384]{0:T(512)S(1)} copy-done((s32[384]{0:T(512)S(1)}, s32[384]{0:T(512)}, u32[]{:S(2)}) %copy-start) | copy-done | bytes 1560
  0.7 32.5 %shard_map.55 = bf16[512,768]{1,0:T(8,128)(2,1)S(1)} custom-call(bf16[384,384]{1,0:T(8,128)(2,1)} %features_in.1, s32[384]{0:T(512)S(1)} %copy-done, bf16[768,768]{1,0:T(8,128)(2,1)} %w_in_in.1, bf16[768,768]{1,0:T(8,128)(2,1)} %w_out_in.1, bf16[512,384]{1,0:T(8,128)(2,1)} %old_in.1), custom_call_target="tpu_custom_call" | custom-call | tf_op jit(solution)/shard_map/pallas_call | solution.py:301
  33.2 0.9 %copy.7 = bf16[512,768]{1,0:T(8,128)(2,1)} copy(bf16[512,768]{1,0:T(8,128)(2,1)S(1)} %shard_map.55) | data formatting | bytes 1572864
Async XLA Ops:
  0.0 0.7 %copy-start = (s32[384]{0:T(512)S(1)}, s32[384]{0:T(512)}, u32[]{:S(2)}) copy-start(s32[384]{0:T(512)} %ids_ref.1) | copy-start | bytes 4612
